TPU v7x, 32 devices: a whole 2x2x4 slice. The times are simulated.
32 devices in a mesh: chan: 8 (over z, y), min: 4 (over x, core).
Axes of the slice: x: 2, y: 2, z: 4, core: 2. Of those that a mesh axis runs over, the one named last changes fastest.
Arguments:
- spectra: bfloat16 [2, 32, 128, 2048], P(None, None, 'min', 'chan'), may hold values from -6 to 6
Outputs:
- cross: float32 [2, 32, 2048, 768], P(None, 'min', 'chan')
All inputs are finite; a program needn't handle non-finite values.
Results may differ from a plain program's by a relative error of at most 0.0027.
Values may be sent and summed in bfloat16 or wider, within the bound.
A program may use at most 64 MiB of HBM per device.

v0:
```python
import jax
import jax.numpy as jnp
from jax import lax
from jax.sharding import PartitionSpec as P

OFFS = 3


water_level = 0.1


def passed_along(array, axis, by):
    length = lax.axis_size(axis)
    return lax.ppermute(array, axis, [(i, (i + by) % length) for i in range(length)])


def whiten(spectra):
    values = spectra.astype(jnp.float32)
    power = values[0] * values[0] + values[1] * values[1]
    level = jnp.mean(power, axis=0, keepdims=True)
    scale = lax.rsqrt(power + water_level * level + 1e-06)
    return (values * scale[None]).astype(jnp.bfloat16)


def partners(white):
    found = [white]
    latest = white
    for step in range(OFFS - 1):
        latest = passed_along(latest, "chan", -1)
        found.append(latest)
    return found


def pair_block(left, partner):
    right_re = jnp.concatenate([partner[0], partner[1]], axis=1)
    right_im = jnp.concatenate([partner[1], -partner[0]], axis=1)
    real_part = jnp.einsum("fmi,fmj->fij", left, right_re, preferred_element_type=jnp.float32)
    imag_part = jnp.einsum("fmi,fmj->fij", left, right_im, preferred_element_type=jnp.float32)
    return (real_part, imag_part)


def on_device(spectra):
    white = whiten(spectra)
    grouped = lax.all_to_all(white, "min", split_axis=1, concat_axis=2, tiled=True)
    blocks_all = partners(grouped)
    own = blocks_all[0]
    left = jnp.concatenate([own[0], own[1]], axis=1)
    real_parts = []
    imag_parts = []
    for partner in blocks_all:
        real_part, imag_part = pair_block(left, partner)
        real_parts.append(real_part)
        imag_parts.append(imag_part)
    windows_all = own.shape[2]
    result = jnp.stack([jnp.concatenate(real_parts, axis=-1), jnp.concatenate(imag_parts, axis=-1)])
    return result * windows_all ** (-0.5)


def solution(mesh):
    return jax.shard_map(
        on_device,
        mesh=mesh,
        in_specs=(P(None, None, "min", "chan"),),
        out_specs=P(None, "min", "chan", None),
        check_vma=False,
    )
```

profile of v0, /device:TPU:0, one launch (start us, length us, event | category | flops | bytes accessed | tf_op | source)
XLA Modules:
  0.0 102.1 jit_solution(15178945849679856373)
XLA Ops:
  0.0 1.5 %copy_convert_fusion = f32[2,32,32,256]{3,2,0,1:T(8,128)S(1)} fusion(bf16[2,32,32,256]{3,2,1,0:T(8,128)(2,1)} %param.1), kind=kLoop, calls=%fused_computation.28 | loop fusion | flops 524288 | bytes 3145728 | tf_op jit(solution)/shard_map/convert_element_type | solution.py:18
  1.5 0.2 fusion.21
  1.7 0.3 rsqrt_bitcast_fusion
  2.0 0.9 copy-done
  2.9 0.3 multiply_convert_fusion
  3.2 18.5 %all_to_all.18 = bf16[2,32,32,256]{3,2,0,1:T(8,128)(2,1)S(1)} all-to-all(bf16[2,32,32,256]{3,2,0,1:T(8,128)(2,1)S(1)} %multiply_convert_fusion), channel_id=1, replica_groups=mesh['chan'=8,'min'=4] {'min'}, dimensions={1} | all-to-all | bytes 2097152 | tf_op jit(solution)/shard_map/all_to_all | solution.py:44
  21.8 1.3 %copy.45 = bf16[2,8,128,256]{2,3,1,0:T(8,128)(2,1)} copy(bf16[2,8,128,256]{3,2,1,0:T(8,128)(2,1)S(1)} %bitcast.27) | data formatting | bytes 2097152 | tf_op jit(solution)/shard_map/all_to_all | solution.py:44
  23.1 4.6 %collective-permute-start = (bf16[2,8,128,256]{2,3,1,0:T(8,128)(2,1)}, bf16[2,8,128,256]{2,3,1,0:T(8,128)(2,1)S(1)}, u32[]{:S(2)}, u32[]{:S(2)}) collective-permute-start(bf16[2,8,128,256]{2,3,1,0:T(8,128)(2,1)} %copy.45), channel_id=1, source_target_pairs={{0,28},{4,0},{8,4},{12,8},{16,12},{20,16},{24,20},{28,24},{1,29},{... | collective-permute-start | bytes 3145736 | tf_op jit(solution)/shard_map/ppermute | solution.py:14
  27.9 0.3 copy.41
  28.2 0.3 copy.42
  28.5 21.6 %collective-permute-done = bf16[2,8,128,256]{2,3,1,0:T(8,128)(2,1)S(1)} collective-permute-done((bf16[2,8,128,256]{2,3,1,0:T(8,128)(2,1)}, bf16[2,8,128,256]{2,3,1,0:T(8,128)(2,1)S(1)}, u32[]{:S(2)}, u32[]{:S(2)}) %collective-permute-start) | collective-permute-done | bytes 1048608 | tf_op jit(solution)/shard_map/ppermute | solution.py:14
  50.0 5.1 %collective-permute-start.1 = (bf16[2,8,128,256]{2,3,1,0:T(8,128)(2,1)S(1)}, bf16[2,8,128,256]{2,3,1,0:T(8,128)(2,1)S(1)}, u32[]{:S(2)}, u32[]{:S(2)}) collective-permute-start(bf16[2,8,128,256]{2,3,1,0:T(8,128)(2,1)S(1)} %collective-permute-done), channel_id=1, source_target_pairs={{0,28},{4,0},{8,4},{12,8},{16,12},{20,16},{24,20},{28,24},{1,29},{... | collective-permute-start | bytes 3145736 | tf_op jit(solution)/shard_map/ppermute | solution.py:14
  55.1 0.5 fusion.29
  55.6 0.1 neg.9
  55.7 0.5 fusion.9
  56.2 0.5 fusion.1
  56.8 0.5 fusion.13
  57.3 19.0 %collective-permute-done.1 = bf16[2,8,128,256]{2,3,1,0:T(8,128)(2,1)S(1)} collective-permute-done((bf16[2,8,128,256]{2,3,1,0:T(8,128)(2,1)S(1)}, bf16[2,8,128,256]{2,3,1,0:T(8,128)(2,1)S(1)}, u32[]{:S(2)}, u32[]{:S(2)}) %collective-permute-start.1) | collective-permute-done | bytes 1048608 | tf_op jit(solution)/shard_map/ppermute | solution.py:14
  76.2 0.1 slice_bitcast_fusion.1
  76.3 0.5 fusion.5
  76.9 0.5 fusion.17
  77.3 3.5 %maximum_bitcast_fusion = (f32[1,8,256,768]{2,3,1,0:T(8,128)S(1)}, f32[1,8,256,768]{2,3,1,0:T(8,128)}) fusion(f32[8,256,256]{1,2,0:T(8,128)S(1)} %fusion.5, f32[8,256,256]{1,2,0:T(8,128)S(1)} %fusion.1, f32[8,256,256]{1,2,0:T(8,128)S(1)} %fusion.29, f32[8,256,256]{1,2,0:T(8,128)S(1)} %fusion.17, f32[8,256,256]{1,2,0:T(8,128)S(1)} %fusion.13, ...), kind=kLoop, calls=%fused_computation.1 | loop fusion | flops 6291456 | bytes 25165824 | tf_op jit(solution)/shard_map/stack | solution.py:55
  80.8 8.7 %maximum_multiply_fusion = f32[2,8,256,768]{2,3,1,0:T(8,128)} fusion(f32[1,8,256,768]{2,3,1,0:T(8,128)} %get-tuple-element.12, f32[1,8,256,768]{2,3,1,0:T(8,128)S(1)} %get-tuple-element.11), kind=kLoop, calls=%fused_computation | loop fusion | flops 6291456 | bytes 25165824 | tf_op jit(solution)/shard_map/mul | solution.py:56
  89.5 12.6 %copy.53 = f32[2,8,256,768]{3,2,1,0:T(8,128)} copy(f32[2,8,256,768]{2,3,1,0:T(8,128)} %maximum_multiply_fusion) | data formatting | bytes 25165824 | tf_op jit(solution)/shard_map/mul | solution.py:56
  (10 shorter events, 0.5 us)
Async XLA Ops:
  1.7 1.2 %copy-start = (bf16[2,32,32,256]{3,2,1,0:T(8,128)(2,1)S(1)}, bf16[2,32,32,256]{3,2,1,0:T(8,128)(2,1)}, u32[]{:S(2)}) copy-start(bf16[2,32,32,256]{3,2,1,0:T(8,128)(2,1)} %param.1) | copy-start | bytes 3145732
  23.1 26.9 %collective-permute-start = (bf16[2,8,128,256]{2,3,1,0:T(8,128)(2,1)}, bf16[2,8,128,256]{2,3,1,0:T(8,128)(2,1)S(1)}, u32[]{:S(2)}, u32[]{:S(2)}) collective-permute-start(bf16[2,8,128,256]{2,3,1,0:T(8,128)(2,1)} %copy.45), channel_id=1, source_target_pairs={{0,28},{4,0},{8,4},{12,8},{16,12},{20,16},{24,20},{28,24},{1,29},{... | collective-permute-start | bytes 3145736 | tf_op jit(solution)/shard_map/ppermute | solution.py:14
  50.0 26.2 %collective-permute-start.1 = (bf16[2,8,128,256]{2,3,1,0:T(8,128)(2,1)S(1)}, bf16[2,8,128,256]{2,3,1,0:T(8,128)(2,1)S(1)}, u32[]{:S(2)}, u32[]{:S(2)}) collective-permute-start(bf16[2,8,128,256]{2,3,1,0:T(8,128)(2,1)S(1)} %collective-permute-done), channel_id=1, source_target_pairs={{0,28},{4,0},{8,4},{12,8},{16,12},{20,16},{24,20},{28,24},{1,29},{... | collective-permute-start | bytes 3145736 | tf_op jit(solution)/shard_map/ppermute | solution.py:14
where the time goes:
time: 103 us; the launch traced here: 102 us
  waiting for transfers between devices  40.5 us (39%)
  blocking collectives  18.5 us (18%)
  local copies, waits for them, and re-layouts  15.8 us (15%)
  other arithmetic  14.7 us (14%)
  starting transfers between devices  9.63 us (9%)
  matrix products  2.82 us (3%)
    ppermute x2, waiting for transfers between devices, passed_along(): lax.ppermute(array, axis, [(i, (i + by) % length) for i in range(length)])  40.5 us
    all_to_all x1, blocking collectives, on_device(): lax.all_to_all(white, 'min', split_axis=1, concat_axis=2, tiled=True)  18.5 us
    mul x1, local copies, waits for them, and re-layouts, on_device(): return result * windows_all ** (-0.5)  12.6 us
    ppermute x2, starting transfers between devices, passed_along(): lax.ppermute(array, axis, [(i, (i + by) % length) for i in range(length)])  9.63 us
    mul x1, other arithmetic, on_device(): return result * windows_all ** (-0.5)  8.71 us
    another operation x1, other arithmetic, on_device(): jnp.stack([jnp.concatenate(real_parts, axis=-1), jnp.concatenate(imag_par...  3.46 us
  transfers between devices with their start and end apart: 2, of which 2 were waited for; matrix products, arithmetic and copies ran while one was open for 3% of the time, Pallas kernels for 0%

commit v1 on v0

v1 whole, which is shorter than its diff:
```python
import functools

import jax
import jax.numpy as jnp
from jax import lax
from jax.experimental import pallas as pl
from jax.experimental.pallas import tpu as pltpu
from jax.sharding import PartitionSpec as P

OFFS = 3
AHEAD = 3
LAG = 2

water_level = 0.1

MESH = pl.DeviceIdType.MESH


def exchange_kernel(n_min, n_chan, s_ref, a_ref, white, power, level,
                    x_send, x_recv, z_send, z_recv, y_send, y_recv):
    bins = a_ref.shape[1]
    all_bins = s_ref.shape[1]
    me = lax.axis_index("min")
    block = lax.axis_index("chan")
    odd = lax.rem(block, 2)
    before2 = lax.rem(block + n_chan - 2, n_chan)
    after2 = lax.rem(block + 2, n_chan)
    pair = block + 1 - 2 * odd

    barrier = pltpu.get_barrier_semaphore()
    for r in range(1, n_min):
        pl.semaphore_signal(barrier, inc=1, device_id=(block, lax.rem(me + r, n_min)), device_id_type=MESH)
    for other in (before2, after2, pair):
        pl.semaphore_signal(barrier, inc=1, device_id=(other, me), device_id_type=MESH)

    level[...] = jnp.zeros_like(level)

    def add_power(b, carry):
        re = s_ref[0, b].astype(jnp.float32)
        im = s_ref[1, b].astype(jnp.float32)
        p = re * re + im * im
        power[b] = p
        level[...] += p
        return carry

    lax.fori_loop(0, all_bins, add_power, 0, unroll=8)
    level[...] = level[...] * (water_level / all_bins) + 1e-06

    pl.semaphore_wait(barrier, n_min - 1 + 3)

    def x_copy(f, r):
        return pltpu.make_async_remote_copy(
            src_ref=white.at[f, r - 1], dst_ref=a_ref.at[0, f, me],
            send_sem=x_send.at[f, r - 1], recv_sem=x_recv.at[f, r - 1],
            device_id=(block, lax.rem(me + r, n_min)), device_id_type=MESH)

    def z_copy(f):
        return pltpu.make_async_remote_copy(
            src_ref=a_ref.at[0, f], dst_ref=a_ref.at[2, f],
            send_sem=z_send.at[f], recv_sem=z_recv.at[f],
            device_id=(before2, me), device_id_type=MESH)

    def y_copy(f, slot):
        return pltpu.make_async_remote_copy(
            src_ref=a_ref.at[slot, f], dst_ref=a_ref.at[1, f],
            send_sem=y_send.at[f], recv_sem=y_recv.at[f],
            device_id=(pair, me), device_id_type=MESH)

    def whiten(f):
        for r in list(range(1, n_min)) + [0]:
            b = lax.rem(me + r, n_min) * bins + f
            scale = lax.rsqrt(power[b] + level[...])
            for part in range(2):
                value = (s_ref[part, b].astype(jnp.float32) * scale).astype(jnp.bfloat16)
                if r:
                    white[f, r - 1, part] = value
                else:
                    a_ref[0, f, me, part] = value
            if r:
                x_copy(f, r).start()

    ahead = min(AHEAD, bins)
    lag = min(LAG, bins)

    def first(f, carry):
        whiten(f)
        return carry

    lax.fori_loop(0, ahead, first, 0)

    def step(f, carry):
        @pl.when(f < bins)
        def _():
            for r in range(1, n_min):
                x_copy(f, r).wait_recv()
            z_copy(f).start()

            @pl.when(odd == 1)
            def _():
                y_copy(f, 0).start()

        @pl.when(f + ahead < bins)
        def _():
            whiten(f + ahead)

        @pl.when(f >= lag)
        def _():
            z_copy(f - lag).wait_recv()

            @pl.when(odd == 0)
            def _():
                y_copy(f - lag, 2).start()

        return carry

    lax.fori_loop(0, bins + lag, step, 0)

    def last(f, carry):
        for r in range(1, n_min):
            x_copy(f, r).wait_send()
        z_copy(f).wait_send()
        y_copy(f, 0).wait_send()
        y_copy(f, 0).wait_recv()
        return carry

    lax.fori_loop(0, bins, last, 0)


def exchange(spectra, n_min, n_chan):
    _, all_bins, windows, channels = spectra.shape
    bins = all_bins // n_min
    return pl.pallas_call(
        functools.partial(exchange_kernel, n_min, n_chan),
        out_shape=jax.ShapeDtypeStruct((OFFS, bins, n_min, 2, windows, channels), jnp.bfloat16),
        in_specs=[pl.BlockSpec(memory_space=pltpu.VMEM)],
        out_specs=pl.BlockSpec(memory_space=pltpu.VMEM),
        scratch_shapes=[
            pltpu.VMEM((bins, n_min - 1, 2, windows, channels), jnp.bfloat16),
            pltpu.VMEM((all_bins, windows, channels), jnp.float32),
            pltpu.VMEM((windows, channels), jnp.float32),
            pltpu.SemaphoreType.DMA((bins, n_min - 1)),
            pltpu.SemaphoreType.DMA((bins, n_min - 1)),
            pltpu.SemaphoreType.DMA((bins,)),
            pltpu.SemaphoreType.DMA((bins,)),
            pltpu.SemaphoreType.DMA((bins,)),
            pltpu.SemaphoreType.DMA((bins,)),
        ],
        compiler_params=pltpu.CompilerParams(
            collective_id=0, has_side_effects=True, vmem_limit_bytes=24 * 2 ** 20),
    )(spectra)


def stack_kernel(scale, a_ref, o_ref):
    _, _, n_min, _, windows, channels = a_ref.shape
    depth = n_min * 2 * windows
    own = a_ref[0, 0]
    turned = jnp.concatenate([-own[:, 1:2], own[:, 0:1]], axis=1)
    left = jnp.concatenate(
        [own.reshape(depth, channels), turned.reshape(depth, channels)], axis=1).T
    for k in range(OFFS):
        right = a_ref[k, 0].reshape(depth, channels)
        both = jnp.dot(left, right, preferred_element_type=jnp.float32) * scale
        o_ref[0, 0, :, k * channels:(k + 1) * channels] = both[:channels]
        o_ref[1, 0, :, k * channels:(k + 1) * channels] = both[channels:]


def stack(blocks):
    _, bins, n_min, _, windows, channels = blocks.shape
    return pl.pallas_call(
        functools.partial(stack_kernel, (n_min * windows) ** -0.5),
        out_shape=jax.ShapeDtypeStruct((2, bins, channels, OFFS * channels), jnp.float32),
        grid=(bins,),
        in_specs=[pl.BlockSpec((OFFS, 1, n_min, 2, windows, channels), lambda f: (0, f, 0, 0, 0, 0))],
        out_specs=pl.BlockSpec((2, 1, channels, OFFS * channels), lambda f: (0, f, 0, 0)),
        compiler_params=pltpu.CompilerParams(
            dimension_semantics=("arbitrary",), vmem_limit_bytes=32 * 2 ** 20),
    )(blocks)


def solution(mesh):
    n_min, n_chan = mesh.shape["min"], mesh.shape["chan"]

    def on_device(spectra):
        return stack(exchange(spectra, n_min, n_chan))

    return jax.shard_map(
        on_device,
        mesh=mesh,
        in_specs=(P(None, None, "min", "chan"),),
        out_specs=P(None, "min", "chan", None),
        check_vma=False,
    )
```

time: 103 us -> 44.7 us (0.43)
  Pallas kernels: 0 us -> 43.1 us
  waiting for transfers between devices: 40.5 us -> 0 us
  blocking collectives: 18.5 us -> 0 us
  other arithmetic: 14.7 us -> 0 us
  local copies, waits for them, and re-layouts: 15.8 us -> 1.22 us
  starting transfers between devices: 9.63 us -> 0 us
  matrix products: 2.82 us -> 0 us
    pallas_call x0 -> x2, Pallas kernels: none -> 43.1 us  [the longest x1 36.2 us: exchange(): pl.pallas_call(functools.partial(exchange_kernel, n_min, n_chan), out_sha...]
    ppermute x2 -> x0, waiting for transfers between devices: 40.5 us -> none  [passed_along(): lax.ppermute(array, axis, [(i, (i + by) % length) for i in range(length)])]
    all_to_all x1 -> x0, blocking collectives: 18.5 us -> none  [on_device(): lax.all_to_all(white, 'min', split_axis=1, concat_axis=2, tiled=True)]
    mul x1 -> x0, local copies, waits for them, and re-layouts: 12.6 us -> none  [on_device(): return result * windows_all ** (-0.5)]
    ppermute x2 -> x0, starting transfers between devices: 9.63 us -> none  [passed_along(): lax.ppermute(array, axis, [(i, (i + by) % length) for i in range(length)])]
    mul x3 -> x0, other arithmetic: 8.99 us -> none  [the longest x1 8.71 us: on_device(): return result * windows_all ** (-0.5)]
    another operation x1 -> x0, other arithmetic: 3.46 us -> none  [on_device(): jnp.stack([jnp.concatenate(real_parts, axis=-1), jnp.concatenate(imag_par...]
    dot_general x6 -> x0, matrix products: 2.82 us -> none  [the longest x3 1.41 us: pair_block(): jnp.einsum('fmi,fmj->fij', left, right_im, preferred_element_type=jnp.flo...]
  transfers between devices with their start and end apart: 2 -> 0, of which waited for: 2 -> 0; matrix products, arithmetic and copies ran while one was open for 3% -> 0% of each run, Pallas kernels for 0% -> 0%
where the time goes in v1:
time: 44.7 us; the launch traced here: 44.3 us
  Pallas kernels  43.1 us (96%)
  local copies, waits for them, and re-layouts  1.22 us (3%)
    pallas_call x1, Pallas kernels, exchange(): pl.pallas_call(functools.partial(exchange_kernel, n_min, n_chan), out_sha...  36.2 us
    pallas_call x1, Pallas kernels, stack(): pl.pallas_call(functools.partial(stack_kernel, (n_min * windows) ** (-0.5...  6.89 us
    unnamed x2, local copies, waits for them, and re-layouts  1.22 us

profile of v1, /device:TPU:0, one launch (start us, length us, event | category | flops | bytes accessed | tf_op | source)
XLA Modules:
  0.0 44.3 jit_solution(1287768857082656523)
XLA Ops:
  0.0 0.0 copy-start
  0.0 1.2 %copy-done = bf16[2,32,32,256]{3,2,1,0:T(8,128)(2,1)S(1)} copy-done((bf16[2,32,32,256]{3,2,1,0:T(8,128)(2,1)S(1)}, bf16[2,32,32,256]{3,2,1,0:T(8,128)(2,1)}, u32[]{:S(2)}) %copy-start) | copy-done | bytes 1048600
  1.2 36.2 %shard_map.17.a_ref = bf16[3,8,4,2,32,256]{5,4,3,2,1,0:T(8,128)(2,1)S(1)} custom-call(bf16[2,32,32,256]{3,2,1,0:T(8,128)(2,1)S(1)} %copy-done), custom_call_target="tpu_custom_call" | custom-call | tf_op jit(solution)/shard_map/pallas_call | solution.py:132
  37.5 6.9 %shard_map.18 = f32[2,8,256,768]{3,2,1,0:T(8,128)} custom-call(bf16[3,8,4,2,32,256]{5,4,3,2,1,0:T(8,128)(2,1)S(1)} %shard_map.17.a_ref), custom_call_target="tpu_custom_call" | custom-call | tf_op jit(solution)/shard_map/pallas_call | solution.py:169
Async XLA Ops:
  0.0 1.2 %copy-start = (bf16[2,32,32,256]{3,2,1,0:T(8,128)(2,1)S(1)}, bf16[2,32,32,256]{3,2,1,0:T(8,128)(2,1)}, u32[]{:S(2)}) copy-start(bf16[2,32,32,256]{3,2,1,0:T(8,128)(2,1)} %s_ref.1) | copy-start | bytes 3145732

commit v2 on v1

v2 whole, which is shorter than its diff:
```python
import functools

import jax
import jax.numpy as jnp
from jax import lax
from jax.experimental import pallas as pl
from jax.experimental.pallas import tpu as pltpu
from jax.sharding import PartitionSpec as P

OFFS = 3
AHEAD = 3
LAG = 2

water_level = 0.1

MESH = pl.DeviceIdType.MESH


def flipped(index, bits, size):
    result, weight = index, 1
    while weight < size:
        if bits & weight:
            result = result + weight * (1 - 2 * lax.rem(index // weight, 2))
        weight *= 2
    return result


def stacked_kernel(n_min, n_chan, s_ref, o_ref, a_ref, left, white, power, level,
                    x_send, x_recv, z_send, z_recv, y_send, y_recv):
    bins = a_ref.shape[1]
    pairs = n_min // 2
    _, all_bins, windows, channels = s_ref.shape
    depth = n_min * 2 * windows
    norm = (n_min * windows) ** -0.5
    me = lax.axis_index("min")
    block = lax.axis_index("chan")
    odd = lax.rem(block, 2)
    before2 = lax.rem(block + n_chan - 2, n_chan)
    after2 = lax.rem(block + 2, n_chan)
    pair = block + 1 - 2 * odd

    barrier = pltpu.get_barrier_semaphore()
    for r in range(1, n_min):
        pl.semaphore_signal(barrier, inc=1, device_id=(block, flipped(me, r, n_min)), device_id_type=MESH)
    for other in (before2, after2, pair):
        pl.semaphore_signal(barrier, inc=1, device_id=(other, me), device_id_type=MESH)

    level[...] = jnp.zeros_like(level)

    def add_power(b, carry):
        re = s_ref[0, b].astype(jnp.float32)
        im = s_ref[1, b].astype(jnp.float32)
        p = re * re + im * im
        power[b] = p
        level[...] += p
        return carry

    lax.fori_loop(0, all_bins, add_power, 0, unroll=8)
    level[...] = level[...] * (water_level / all_bins) + 1e-06

    pl.semaphore_wait(barrier, n_min - 1 + 3)

    def x_copy(f, r):
        return pltpu.make_async_remote_copy(
            src_ref=white.at[f, r - 1], dst_ref=a_ref.at[0, f, me],
            send_sem=x_send.at[f, r - 1], recv_sem=x_recv.at[f, r - 1],
            device_id=(block, flipped(me, r, n_min)), device_id_type=MESH)

    def of_pair(q):
        return pl.ds(2 * flipped(me // 2, q, pairs), 2)

    def z_copy(f, q):
        return pltpu.make_async_remote_copy(
            src_ref=a_ref.at[0, f, of_pair(q)], dst_ref=a_ref.at[2, f, of_pair(q)],
            send_sem=z_send.at[f, q], recv_sem=z_recv.at[f, q],
            device_id=(before2, me), device_id_type=MESH)

    def y_copy(f, q, slot):
        return pltpu.make_async_remote_copy(
            src_ref=a_ref.at[slot, f, of_pair(q)], dst_ref=a_ref.at[1, f, of_pair(q)],
            send_sem=y_send.at[f, q], recv_sem=y_recv.at[f, q],
            device_id=(pair, me), device_id_type=MESH)

    def whiten(f):
        for r in list(range(2, n_min)) + [1, 0]:
            b = flipped(me, r, n_min) * bins + f
            scale = lax.rsqrt(power[b] + level[...])
            for part in range(2):
                value = (s_ref[part, b].astype(jnp.float32) * scale).astype(jnp.bfloat16)
                if r:
                    white[f, r - 1, part] = value
                else:
                    a_ref[0, f, me, part] = value
            if r:
                x_copy(f, r).start()

    ahead = min(AHEAD, bins)
    lag = min(LAG, bins)

    def first(f, carry):
        whiten(f)
        return carry

    lax.fori_loop(0, ahead, first, 0)

    def pass_on(f, q):
        z_copy(f, q).start()

        @pl.when(odd == 1)
        def _():
            y_copy(f, q, 0).start()

    def turn(f):
        own = a_ref[0, f]
        turned = jnp.concatenate([-own[:, 1:2], own[:, 0:1]], axis=1)
        left[f] = jnp.concatenate(
            [own.reshape(depth, channels), turned.reshape(depth, channels)], axis=1).T

    def multiply(f, k):
        both = jnp.dot(left[f], a_ref[k, f].reshape(depth, channels),
                       preferred_element_type=jnp.float32) * norm
        o_ref[0, f, :, k * channels:(k + 1) * channels] = both[:channels]
        o_ref[1, f, :, k * channels:(k + 1) * channels] = both[channels:]

    def step(f, carry):
        @pl.when(f < bins)
        def _():
            x_copy(f, 1).wait_recv()
            pass_on(f, 0)

        @pl.when(f + ahead < bins)
        def _():
            whiten(f + ahead)

        @pl.when((f >= 1) & (f <= bins))
        def _():
            for q in range(1, pairs):
                x_copy(f - 1, 2 * q).wait_recv()
                x_copy(f - 1, 2 * q + 1).wait_recv()
                pass_on(f - 1, q)
            turn(f - 1)
            multiply(f - 1, 0)

        @pl.when((f >= lag) & (f < bins + lag))
        def _():
            for q in range(pairs):
                z_copy(f - lag, q).wait_recv()

                @pl.when(odd == 0)
                def _():
                    y_copy(f - lag, q, 2).start()

            multiply(f - lag, 2)

        @pl.when(f >= lag + 1)
        def _():
            for q in range(pairs):
                y_copy(f - lag - 1, q, 0).wait_recv()
            multiply(f - lag - 1, 1)

        return carry

    lax.fori_loop(0, bins + lag + 1, step, 0)

    def last(f, carry):
        for r in range(1, n_min):
            x_copy(f, r).wait_send()
        for q in range(pairs):
            z_copy(f, q).wait_send()
            y_copy(f, q, 0).wait_send()
        return carry

    lax.fori_loop(0, bins, last, 0)


def stacked(spectra, n_min, n_chan):
    _, all_bins, windows, channels = spectra.shape
    bins = all_bins // n_min
    return pl.pallas_call(
        functools.partial(stacked_kernel, n_min, n_chan),
        out_shape=jax.ShapeDtypeStruct((2, bins, channels, OFFS * channels), jnp.float32),
        in_specs=[pl.BlockSpec(memory_space=pltpu.VMEM)],
        out_specs=pl.BlockSpec(memory_space=pltpu.VMEM),
        scratch_shapes=[
            pltpu.VMEM((OFFS, bins, n_min, 2, windows, channels), jnp.bfloat16),
            pltpu.VMEM((bins, 2 * channels, n_min * 2 * windows), jnp.bfloat16),
            pltpu.VMEM((bins, n_min - 1, 2, windows, channels), jnp.bfloat16),
            pltpu.VMEM((all_bins, windows, channels), jnp.float32),
            pltpu.VMEM((windows, channels), jnp.float32),
            pltpu.SemaphoreType.DMA((bins, n_min - 1)),
            pltpu.SemaphoreType.DMA((bins, n_min - 1)),
            pltpu.SemaphoreType.DMA((bins, n_min // 2)),
            pltpu.SemaphoreType.DMA((bins, n_min // 2)),
            pltpu.SemaphoreType.DMA((bins, n_min // 2)),
            pltpu.SemaphoreType.DMA((bins, n_min // 2)),
        ],
        compiler_params=pltpu.CompilerParams(
            collective_id=0, has_side_effects=True, vmem_limit_bytes=24 * 2 ** 20),
    )(spectra)


def write_kernel(v_ref, o_ref, sem):
    def copy(part, f):
        return pltpu.make_async_copy(v_ref.at[part, f], o_ref.at[part, f], sem.at[part, f])

    both = [(part, f) for f in range(v_ref.shape[1]) for part in range(2)]
    for at in both:
        copy(*at).start()
    for at in both:
        copy(*at).wait()


def written(result):
    return pl.pallas_call(
        write_kernel,
        out_shape=jax.ShapeDtypeStruct(result.shape, result.dtype),
        in_specs=[pl.BlockSpec(memory_space=pltpu.VMEM)],
        out_specs=pl.BlockSpec(memory_space=pl.ANY),
        scratch_shapes=[pltpu.SemaphoreType.DMA(result.shape[:2])],
        compiler_params=pltpu.CompilerParams(vmem_limit_bytes=24 * 2 ** 20),
    )(result)


def solution(mesh):
    n_min, n_chan = mesh.shape["min"], mesh.shape["chan"]

    def on_device(spectra):
        return written(stacked(spectra, n_min, n_chan))

    return jax.shard_map(
        on_device,
        mesh=mesh,
        in_specs=(P(None, None, "min", "chan"),),
        out_specs=P(None, "min", "chan", None),
        check_vma=False,
    )
```

time: 44.7 us -> 41.1 us (0.919)
  Pallas kernels: 43.1 us -> 39.6 us
    pallas_call x2, Pallas kernels: 43.1 us -> 39.6 us  [the longest x1 34.9 us: stacked(): pl.pallas_call(functools.partial(stacked_kernel, n_min, n_chan), out_shap...]
where the time goes in v2:
time: 41.1 us; the launch traced here: 40.9 us
  Pallas kernels  39.6 us (96%)
  local copies, waits for them, and re-layouts  1.22 us (3%)
    pallas_call x1, Pallas kernels, stacked(): pl.pallas_call(functools.partial(stacked_kernel, n_min, n_chan), out_shap...  34.9 us
    pallas_call x1, Pallas kernels, written(): pl.pallas_call(write_kernel, out_shape=jax.ShapeDtypeStruct(result.shape,...  4.7 us
    unnamed x2, local copies, waits for them, and re-layouts  1.22 us

profile of v2, /device:TPU:0, one launch (start us, length us, event | category | flops | bytes accessed | tf_op | source)
XLA Modules:
  0.0 40.9 jit_solution(6515935486466178334)
XLA Ops:
  0.0 0.0 copy-start
  0.0 1.2 %copy-done = bf16[2,32,32,256]{3,2,1,0:T(8,128)(2,1)S(1)} copy-done((bf16[2,32,32,256]{3,2,1,0:T(8,128)(2,1)S(1)}, bf16[2,32,32,256]{3,2,1,0:T(8,128)(2,1)}, u32[]{:S(2)}) %copy-start) | copy-done | bytes 1048600
  1.2 34.9 %shard_map.17.v_ref = f32[2,8,256,768]{3,2,1,0:T(8,128)S(1)} custom-call(bf16[2,32,32,256]{3,2,1,0:T(8,128)(2,1)S(1)} %copy-done), custom_call_target="tpu_custom_call" | custom-call | tf_op jit(solution)/shard_map/pallas_call | solution.py:179
  36.2 4.7 %shard_map.18 = f32[2,8,256,768]{3,2,1,0:T(8,128)} custom-call(f32[2,8,256,768]{3,2,1,0:T(8,128)S(1)} %shard_map.17.v_ref), custom_call_target="tpu_custom_call" | custom-call | tf_op jit(solution)/shard_map/pallas_call | solution.py:214
Async XLA Ops:
  0.0 1.2 %copy-start = (bf16[2,32,32,256]{3,2,1,0:T(8,128)(2,1)S(1)}, bf16[2,32,32,256]{3,2,1,0:T(8,128)(2,1)}, u32[]{:S(2)}) copy-start(bf16[2,32,32,256]{3,2,1,0:T(8,128)(2,1)} %s_ref.1) | copy-start | bytes 3145732

commit v3 on v2

--- a/solution.py
+++ b/solution.py
@@ -8,7 +8,7 @@
 from jax.sharding import PartitionSpec as P
 
 OFFS = 3
-AHEAD = 3
+AHEAD = 1
 LAG = 2
 
 water_level = 0.1
@@ -122,6 +122,13 @@
         o_ref[0, f, :, k * channels:(k + 1) * channels] = both[:channels]
         o_ref[1, f, :, k * channels:(k + 1) * channels] = both[channels:]
 
+    def forward(f, q):
+        z_copy(f, q).wait_recv()
+
+        @pl.when(odd == 0)
+        def _():
+            y_copy(f, q, 2).start()
+
     def step(f, carry):
         @pl.when(f < bins)
         def _():
@@ -138,18 +145,14 @@
                 x_copy(f - 1, 2 * q).wait_recv()
                 x_copy(f - 1, 2 * q + 1).wait_recv()
                 pass_on(f - 1, q)
+            forward(f - 1, 0)
             turn(f - 1)
             multiply(f - 1, 0)
 
         @pl.when((f >= lag) & (f < bins + lag))
         def _():
-            for q in range(pairs):
-                z_copy(f - lag, q).wait_recv()
-
-                @pl.when(odd == 0)
-                def _():
-                    y_copy(f - lag, q, 2).start()
-
+            for q in range(1, pairs):
+                forward(f - lag, q)
             multiply(f - lag, 2)
 
         @pl.when(f >= lag + 1)

time: 41.1 us -> 39.1 us (0.951)
  Pallas kernels: 39.6 us -> 37.7 us
    pallas_call x1, Pallas kernels: 34.9 us -> 33 us  [stacked(): pl.pallas_call(functools.partial(stacked_kernel, n_min, n_chan), out_shap...]
where the time goes in v3:
time: 39.1 us; the launch traced here: 38.9 us
  Pallas kernels  37.7 us (96%)
  local copies, waits for them, and re-layouts  1.22 us (3%)
    pallas_call x1, Pallas kernels, stacked(): pl.pallas_call(functools.partial(stacked_kernel, n_min, n_chan), out_shap...  33 us
    pallas_call x1, Pallas kernels, written(): pl.pallas_call(write_kernel, out_shape=jax.ShapeDtypeStruct(result.shape,...  4.7 us
    unnamed x2, local copies, waits for them, and re-layouts  1.22 us

profile of v3, /device:TPU:0, one launch (start us, length us, event | category | flops | bytes accessed | tf_op | source)
XLA Modules:
  0.0 38.9 jit_solution(3215660829064086208)
XLA Ops:
  0.0 0.0 copy-start
  0.0 1.2 %copy-done = bf16[2,32,32,256]{3,2,1,0:T(8,128)(2,1)S(1)} copy-done((bf16[2,32,32,256]{3,2,1,0:T(8,128)(2,1)S(1)}, bf16[2,32,32,256]{3,2,1,0:T(8,128)(2,1)}, u32[]{:S(2)}) %copy-start) | copy-done | bytes 1048600
  1.2 33.0 %shard_map.17.v_ref = f32[2,8,256,768]{3,2,1,0:T(8,128)S(1)} custom-call(bf16[2,32,32,256]{3,2,1,0:T(8,128)(2,1)S(1)} %copy-done), custom_call_target="tpu_custom_call" | custom-call | tf_op jit(solution)/shard_map/pallas_call | solution.py:182
  34.2 4.7 %shard_map.18 = f32[2,8,256,768]{3,2,1,0:T(8,128)} custom-call(f32[2,8,256,768]{3,2,1,0:T(8,128)S(1)} %shard_map.17.v_ref), custom_call_target="tpu_custom_call" | custom-call | tf_op jit(solution)/shard_map/pallas_call | solution.py:217
Async XLA Ops:
  0.0 1.2 %copy-start = (bf16[2,32,32,256]{3,2,1,0:T(8,128)(2,1)S(1)}, bf16[2,32,32,256]{3,2,1,0:T(8,128)(2,1)}, u32[]{:S(2)}) copy-start(bf16[2,32,32,256]{3,2,1,0:T(8,128)(2,1)} %s_ref.1) | copy-start | bytes 3145732

commit v4 on v3

--- a/solution.py
+++ b/solution.py
@@ -45,18 +45,15 @@
     for other in (before2, after2, pair):
         pl.semaphore_signal(barrier, inc=1, device_id=(other, me), device_id_type=MESH)
 
-    level[...] = jnp.zeros_like(level)
-
     def add_power(b, carry):
         re = s_ref[0, b].astype(jnp.float32)
         im = s_ref[1, b].astype(jnp.float32)
         p = re * re + im * im
         power[b] = p
-        level[...] += p
-        return carry
-
-    lax.fori_loop(0, all_bins, add_power, 0, unroll=8)
-    level[...] = level[...] * (water_level / all_bins) + 1e-06
+        return carry + p
+
+    total = lax.fori_loop(0, all_bins, add_power, jnp.zeros(level.shape, jnp.float32), unroll=8)
+    level[...] = total * (water_level / all_bins) + 1e-06
 
     pl.semaphore_wait(barrier, n_min - 1 + 3)
 
@@ -82,7 +79,7 @@
             device_id=(pair, me), device_id_type=MESH)
 
     def whiten(f):
-        for r in list(range(2, n_min)) + [1, 0]:
+        for r in [1, 0] + list(range(2, n_min)):
             b = flipped(me, r, n_min) * bins + f
             scale = lax.rsqrt(power[b] + level[...])
             for part in range(2):

time: 39.1 us -> 39.1 us (level)
  no operation moved by 1% of the time
where the time goes in v4:
time: 39.1 us; the launch traced here: 39 us
  Pallas kernels  37.7 us (96%)
  local copies, waits for them, and re-layouts  1.22 us (3%)
    pallas_call x1, Pallas kernels, stacked(): pl.pallas_call(functools.partial(stacked_kernel, n_min, n_chan), out_shap...  33 us
    pallas_call x1, Pallas kernels, written(): pl.pallas_call(write_kernel, out_shape=jax.ShapeDtypeStruct(result.shape,...  4.7 us
    unnamed x2, local copies, waits for them, and re-layouts  1.22 us

profile of v4, /device:TPU:0, one launch (start us, length us, event | category | flops | bytes accessed | tf_op | source)
XLA Modules:
  0.0 39.0 jit_solution(11947694969700005086)
XLA Ops:
  0.0 0.0 copy-start
  0.0 1.2 %copy-done = bf16[2,32,32,256]{3,2,1,0:T(8,128)(2,1)S(1)} copy-done((bf16[2,32,32,256]{3,2,1,0:T(8,128)(2,1)S(1)}, bf16[2,32,32,256]{3,2,1,0:T(8,128)(2,1)}, u32[]{:S(2)}) %copy-start) | copy-done | bytes 1048600
  1.2 33.0 %shard_map.17.v_ref = f32[2,8,256,768]{3,2,1,0:T(8,128)S(1)} custom-call(bf16[2,32,32,256]{3,2,1,0:T(8,128)(2,1)S(1)} %copy-done), custom_call_target="tpu_custom_call" | custom-call | tf_op jit(solution)/shard_map/pallas_call | solution.py:179
  34.3 4.7 %shard_map.18 = f32[2,8,256,768]{3,2,1,0:T(8,128)} custom-call(f32[2,8,256,768]{3,2,1,0:T(8,128)S(1)} %shard_map.17.v_ref), custom_call_target="tpu_custom_call" | custom-call | tf_op jit(solution)/shard_map/pallas_call | solution.py:214
Async XLA Ops:
  0.0 1.2 %copy-start = (bf16[2,32,32,256]{3,2,1,0:T(8,128)(2,1)S(1)}, bf16[2,32,32,256]{3,2,1,0:T(8,128)(2,1)}, u32[]{:S(2)}) copy-start(bf16[2,32,32,256]{3,2,1,0:T(8,128)(2,1)} %s_ref.1) | copy-start | bytes 3145732

commit v5 on v3

--- a/solution.py
+++ b/solution.py
@@ -135,24 +135,33 @@
             x_copy(f, 1).wait_recv()
             pass_on(f, 0)
 
-        @pl.when(f + ahead < bins)
-        def _():
-            whiten(f + ahead)
-
         @pl.when((f >= 1) & (f <= bins))
         def _():
             for q in range(1, pairs):
                 x_copy(f - 1, 2 * q).wait_recv()
                 x_copy(f - 1, 2 * q + 1).wait_recv()
                 pass_on(f - 1, q)
+
+        @pl.when(f + ahead < bins)
+        def _():
+            whiten(f + ahead)
+
+        @pl.when((f >= 1) & (f <= bins))
+        def _():
             forward(f - 1, 0)
+
+        @pl.when((f >= lag) & (f < bins + lag))
+        def _():
+            for q in range(1, pairs):
+                forward(f - lag, q)
+
+        @pl.when((f >= 1) & (f <= bins))
+        def _():
             turn(f - 1)
             multiply(f - 1, 0)
 
         @pl.when((f >= lag) & (f < bins + lag))
         def _():
-            for q in range(1, pairs):
-                forward(f - lag, q)
             multiply(f - lag, 2)
 
         @pl.when(f >= lag + 1)
@@ -160,6 +169,7 @@
             for q in range(pairs):
                 y_copy(f - lag - 1, q, 0).wait_recv()
             multiply(f - lag - 1, 1)
+
 
         return carry
 

time: 39.1 us -> 39.3 us (level)
  no operation moved by 1% of the time
where the time goes in v5:
time: 39.3 us; the launch traced here: 39.2 us
  Pallas kernels  37.9 us (96%)
  local copies, waits for them, and re-layouts  1.22 us (3%)
    pallas_call x1, Pallas kernels, stacked(): pl.pallas_call(functools.partial(stacked_kernel, n_min, n_chan), out_shap...  33.2 us
    pallas_call x1, Pallas kernels, written(): pl.pallas_call(write_kernel, out_shape=jax.ShapeDtypeStruct(result.shape,...  4.7 us
    unnamed x2, local copies, waits for them, and re-layouts  1.22 us

profile of v5, /device:TPU:0, one launch (start us, length us, event | category | flops | bytes accessed | tf_op | source)
XLA Modules:
  0.0 39.2 jit_solution(5916387991046414510)
XLA Ops:
  0.0 0.0 copy-start
  0.0 1.2 %copy-done = bf16[2,32,32,256]{3,2,1,0:T(8,128)(2,1)S(1)} copy-done((bf16[2,32,32,256]{3,2,1,0:T(8,128)(2,1)S(1)}, bf16[2,32,32,256]{3,2,1,0:T(8,128)(2,1)}, u32[]{:S(2)}) %copy-start) | copy-done | bytes 1048600
  1.2 33.2 %shard_map.17.v_ref = f32[2,8,256,768]{3,2,1,0:T(8,128)S(1)} custom-call(bf16[2,32,32,256]{3,2,1,0:T(8,128)(2,1)S(1)} %copy-done), custom_call_target="tpu_custom_call" | custom-call | tf_op jit(solution)/shard_map/pallas_call | solution.py:192
  34.5 4.7 %shard_map.18 = f32[2,8,256,768]{3,2,1,0:T(8,128)} custom-call(f32[2,8,256,768]{3,2,1,0:T(8,128)S(1)} %shard_map.17.v_ref), custom_call_target="tpu_custom_call" | custom-call | tf_op jit(solution)/shard_map/pallas_call | solution.py:227
Async XLA Ops:
  0.0 1.2 %copy-start = (bf16[2,32,32,256]{3,2,1,0:T(8,128)(2,1)S(1)}, bf16[2,32,32,256]{3,2,1,0:T(8,128)(2,1)}, u32[]{:S(2)}) copy-start(bf16[2,32,32,256]{3,2,1,0:T(8,128)(2,1)} %s_ref.1) | copy-start | bytes 3145732
